TPU v7x, 32 devices: a whole 2x2x4 slice. The times are simulated.
32 devices in a mesh: section: 2 (over x), dp: 4 (over y, core), expert: 4 (over z).
Axes of the slice: x: 2, y: 2, z: 4, core: 2. Of those that a mesh axis runs over, the one named last changes fastest.
Arguments:
- inbound: bfloat16 [2, 16, 256, 1024], P('section', ('dp', 'expert')), may hold values from -6 to 6
- queued: bfloat16 [16, 256, 1024], P(('dp', 'expert')), may hold values from -6 to 6
- routes: int32 [2, 2, 16, 256, 1], P('section', None, ('dp', 'expert')), may hold values from 0 to 3
- first_gain: float32 [2, 1024], P('section'), may hold values from 0.1 to 1.9
- attention_in: bfloat16 [2, 1024, 1536], P('section', 'dp'), may hold values from -3.1875 to 3.1875
- attention_out: bfloat16 [2, 512, 1024], P('section', 'dp'), may hold values from -0.25 to 0.25
- second_gain: float32 [2, 1024], P('section'), may hold values from 0.1 to 1.9
- router: bfloat16 [2, 1024, 4], P('section'), may hold values from -0.375 to 0.375
- expert_in: bfloat16 [2, 4, 1024, 2048], P('section', 'expert', 'dp'), may hold values from -0.1875 to 0.1875
- expert_out: bfloat16 [2, 4, 2048, 1024], P('section', 'expert', 'dp'), may hold values from -0.125 to 0.125
Outputs:
- section_output: bfloat16 [2, 2, 16, 256, 1024], P('section', None, ('dp', 'expert'))
All inputs are finite; a program needn't handle non-finite values.
Results may differ from a plain program's by a relative error of at most 0.0056.
Values may be sent and summed in bfloat16 or wider, within the bound.
A program may use at most 64 MiB of HBM per device.

v0:
```python
from functools import partial

import jax
import jax.numpy as jnp
from jax import lax
from jax.sharding import PartitionSpec as P

HEAD_DIM = 64
CAP = 16


EPSILON = 1e-06


def shifted(shard, axis, by):
    count = lax.axis_size(axis)
    pairs = [(i, i + by) for i in range(count) if 0 <= i + by < count]
    return lax.ppermute(shard, axis, pairs)


def layer_norm(activations, gain_vector):
    widened = activations.astype(jnp.float32)
    centre = widened - jnp.mean(widened, axis=-1, keepdims=True)
    spread = jnp.mean(centre * centre, axis=-1, keepdims=True)
    return (centre * lax.rsqrt(spread + EPSILON) * gain_vector).astype(jnp.bfloat16)


def build_slots(chosen, expert_count):
    onehot = (chosen[:, None] == jnp.arange(expert_count, dtype=jnp.int32)[None, :]).astype(
        jnp.int32
    )
    before = jnp.cumsum(onehot, axis=0) - onehot
    position = jnp.sum(before * onehot, axis=1)
    retained = position < CAP
    slot_index = chosen * CAP + position
    slot_table = (
        slot_index[:, None] == jnp.arange(expert_count * CAP, dtype=jnp.int32)[None, :]
    ) & retained[:, None]
    return (onehot, slot_table, slot_index, retained)


def attend(tokens, gain_vector, project_in, project_out):
    image_count, token_count, model_width = tokens.shape
    head_width = project_out.shape[0]
    head_count = head_width // HEAD_DIM
    normed = layer_norm(tokens, gain_vector)
    mixed_rows = jnp.dot(
        normed.reshape(image_count * token_count, model_width),
        project_in,
        preferred_element_type=jnp.float32,
    ).astype(jnp.bfloat16)
    mixed_rows = mixed_rows.reshape(image_count, token_count, 3, head_count, HEAD_DIM)
    scores = jnp.einsum(
        "ishd,ithd->ihst",
        mixed_rows[:, :, 0],
        mixed_rows[:, :, 1],
        preferred_element_type=jnp.float32,
    ) * HEAD_DIM ** (-0.5)
    softmax_weights = jax.nn.softmax(scores, axis=-1).astype(jnp.bfloat16)
    context = jnp.einsum(
        "ihst,ithd->ishd", softmax_weights, mixed_rows[:, :, 2], preferred_element_type=jnp.float32
    )
    context = context.astype(jnp.bfloat16).reshape(image_count * token_count, head_width)
    branch = jnp.dot(context, project_out, preferred_element_type=jnp.float32).reshape(
        image_count, token_count, model_width
    )
    return (tokens.astype(jnp.float32) + branch).astype(jnp.bfloat16)


def route_and_mix(residual, chosen, gain_vector, router_cols, own_in, own_out):
    image_count, token_count, model_width = residual.shape
    expert_count = router_cols.shape[1]
    normed = layer_norm(residual, gain_vector)
    logits = jnp.dot(
        normed.reshape(image_count * token_count, model_width),
        router_cols,
        preferred_element_type=jnp.float32,
    ).reshape(image_count, token_count, expert_count)
    onehot, slot_table, slot_index, retained = jax.vmap(
        partial(build_slots, expert_count=expert_count)
    )(chosen)
    gating = jax.nn.sigmoid(jnp.sum(logits * onehot.astype(jnp.float32), axis=-1))
    outgoing = jnp.einsum(
        "isk,isd->ikd", slot_table.astype(jnp.bfloat16), normed, preferred_element_type=jnp.float32
    ).astype(jnp.bfloat16)
    outgoing = outgoing.reshape(image_count, expert_count, CAP, model_width)
    arrived = lax.all_to_all(outgoing, "expert", split_axis=1, concat_axis=0, tiled=True)
    flat_rows = arrived.reshape(-1, model_width)
    hidden = jax.nn.gelu(
        jnp.dot(flat_rows, own_in, preferred_element_type=jnp.float32), approximate=False
    ).astype(jnp.bfloat16)
    answer = jnp.dot(hidden, own_out, preferred_element_type=jnp.float32).astype(jnp.bfloat16)
    answered = lax.all_to_all(
        answer.reshape(arrived.shape), "expert", split_axis=0, concat_axis=1, tiled=True
    )
    answered = answered.reshape(image_count, expert_count * CAP, model_width)
    combined = jnp.einsum(
        "isk,ikd->isd",
        slot_table.astype(jnp.bfloat16),
        answered,
        preferred_element_type=jnp.float32,
    )
    return (residual.astype(jnp.float32) + gating[:, :, None] * combined).astype(jnp.bfloat16)


def per_device(
    inbound,
    queued,
    routes,
    first_gain,
    attention_in,
    attention_out,
    second_gain,
    router,
    expert_in,
    expert_out,
):
    section_index = lax.axis_index("section")
    chosen = routes[0, :, :, :, 0]
    full_in, full_out = (
        lax.all_gather(attention_in, "dp", axis=1, tiled=True),
        lax.all_gather(attention_out, "dp", axis=1, tiled=True),
    )
    first_mixed = attend(inbound[0], first_gain[0], full_in[0], full_out[0])
    own_in, own_out = (
        lax.all_gather(expert_in[:, 0], "dp", axis=1, tiled=True),
        lax.all_gather(expert_out[:, 0], "dp", axis=1, tiled=True),
    )
    first_tick = route_and_mix(
        first_mixed, chosen[0], second_gain[0], router[0], own_in[0], own_out[0]
    )
    arrived = shifted(first_tick, "section", 1)
    entering = jnp.where(section_index == 0, queued, arrived)
    second_mixed = attend(entering, first_gain[0], full_in[0], full_out[0])
    second_tick = route_and_mix(
        second_mixed, chosen[1], second_gain[0], router[0], own_in[0], own_out[0]
    )
    return jnp.stack([first_tick, second_tick])[None]


def solution(mesh):
    in_specs = (
        P("section", ("dp", "expert"), None, None),
        P(("dp", "expert"), None, None),
        P("section", None, ("dp", "expert"), None, None),
        P("section", None),
        P("section", "dp", None),
        P("section", "dp", None),
        P("section", None),
        P("section", None, None),
        P("section", "expert", "dp", None),
        P("section", "expert", "dp", None),
    )
    out_specs = P("section", None, ("dp", "expert"), None, None)
    return jax.shard_map(
        per_device, mesh=mesh, in_specs=in_specs, out_specs=out_specs, check_vma=False
    )
```

profile of v0, /device:TPU:0, one launch (start us, length us, event | category | flops | bytes accessed | tf_op | source)
XLA Modules:
  0.0 201.7 jit_solution(5057114900987125693)
XLA Ops:
  6.6 0.7 all-gather.7.cloned.1.call-update
  7.3 0.7 all-gather.9.cloned.1.call-update
  8.1 0.7 all-gather.11.cloned.1.call-update
  9.4 1.2 reduce-window.14
  11.1 1.2 reduce-window.16
  13.0 27.2 %all-gather.7.cloned.1.call-done = bf16[1,1024,1536]{2,1,0:T(8,128)(2,1)} async-done(((bf16[1,256,1536]{2,1,0:T(8,128)(2,1)}), bf16[1,1024,1536]{2,1,0:T(8,128)(2,1)}) %all-gather.7.cloned.1.call-update) | async-done | bytes 3145744 | tf_op jit(solution)/shard_map/all_gather | solution.py:121
  40.2 3.0 %fusion.14 = bf16[256,1536]{1,0:T(8,128)(2,1)S(1)} fusion(bf16[1,1024,1536]{2,1,0:T(8,128)(2,1)} %all-gather.7.cloned.1.call-done, bf16[1,1,256,1024]{3,2,1,0:T(8,128)(2,1)S(1)} %copy-done.1, f32[1024]{0:T(1024)S(1)} %bitcast.238, f32[256]{0:T(256)S(1)} %add_rsqrt_fusion.3, f32[256]{0:T(256)S(1)} %broadcast_multiply_fusion.3), kind=kOutput, calls=%fused_computation.14 | convolution fusion | flops 807010304 | bytes 4462592 | tf_op jit(solution)/shard_map/dot_general | solution.py:47
  43.5 0.8 fusion.262
  44.3 1.1 convolution_convert_fusion.1
  45.4 13.1 %all-gather.9.cloned.1.call-done = bf16[1,512,1024]{2,1,0:T(8,128)(2,1)} async-done(((bf16[1,128,1024]{2,1,0:T(8,128)(2,1)}), bf16[1,512,1024]{2,1,0:T(8,128)(2,1)}) %all-gather.9.cloned.1.call-update) | async-done | bytes 1048592 | tf_op jit(solution)/shard_map/all_gather | solution.py:122
  58.5 1.8 convert_reduce_fusion.3
  60.9 1.0 convolution_convert_fusion.3
  61.9 4.6 %all-to-all-start = ((bf16[1,4,16,1024]{3,2,0,1:T(8,128)(2,1)}), bf16[1,4,16,1024]{3,2,0,1:T(8,128)(2,1)S(1)}, u32[]{:S(2)}, u32[]{:S(2)}) async-start(bf16[1,4,16,1024]{3,2,0,1:T(8,128)(2,1)} %bitcast.22), calls=%async_computation | async-start | bytes 262144 | tf_op jit(solution)/shard_map/all_to_all | solution.py:87
  67.0 5.8 %all-to-all-done = bf16[1,4,16,1024]{3,2,0,1:T(8,128)(2,1)S(1)} async-done(((bf16[1,4,16,1024]{3,2,0,1:T(8,128)(2,1)}), bf16[1,4,16,1024]{3,2,0,1:T(8,128)(2,1)S(1)}, u32[]{:S(2)}, u32[]{:S(2)}) %all-to-all-start) | async-done | bytes 131104 | tf_op jit(solution)/shard_map/all_to_all | solution.py:87
  72.8 21.8 %all-gather.11.cloned.1.call-done = bf16[1,1,1024,2048]{3,2,1,0:T(8,128)(2,1)} async-done(((bf16[1,1,256,2048]{3,2,1,0:T(8,128)(2,1)}), bf16[1,1,1024,2048]{3,2,1,0:T(8,128)(2,1)}) %all-gather.11.cloned.1.call-update) | async-done | bytes 4194320 | tf_op jit(solution)/shard_map/all_gather | solution.py:126
  94.6 35.9 %all-gather.13.cloned.1.call-done = bf16[1,1,2048,1024]{3,2,1,0:T(8,128)(2,1)} async-done(((bf16[1,1,512,1024]{3,2,1,0:T(8,128)(2,1)}), bf16[1,1,2048,1024]{3,2,1,0:T(8,128)(2,1)}) %all-gather.13.cloned.1.call-update) | async-done | bytes 4194320 | tf_op jit(solution)/shard_map/all_gather | solution.py:127
  130.5 6.8 %fusion.34 = bf16[64,1024]{1,0:T(8,128)(2,1)} fusion(bf16[1,1,2048,1024]{3,2,1,0:T(8,128)(2,1)} %all-gather.13.cloned.1.call-done, bf16[64,1024]{1,0:T(8,128)(2,1)S(1)} %bitcast.224, bf16[1,1,1024,2048]{3,2,1,0:T(8,128)(2,1)} %all-gather.11.cloned.1.call-done), kind=kOutput, calls=%fused_computation.55 | convolution fusion | flops 545456128 | bytes 8650752 | tf_op jit(solution)/shard_map/dot_general | solution.py:92
  137.3 4.6 %all-to-all-start.1 = ((bf16[4,1,16,1024]{3,2,1,0:T(8,128)(2,1)}), bf16[4,1,16,1024]{3,2,1,0:T(8,128)(2,1)S(1)}, u32[]{:S(2)}, u32[]{:S(2)}) async-start(bf16[4,1,16,1024]{3,2,1,0:T(8,128)(2,1)} %bitcast.27), calls=%async_computation.1 | async-start | bytes 262144 | tf_op jit(solution)/shard_map/all_to_all | solution.py:93
  142.0 6.3 %all-to-all-done.1 = bf16[4,1,16,1024]{3,2,1,0:T(8,128)(2,1)S(1)} async-done(((bf16[4,1,16,1024]{3,2,1,0:T(8,128)(2,1)}), bf16[4,1,16,1024]{3,2,1,0:T(8,128)(2,1)S(1)}, u32[]{:S(2)}, u32[]{:S(2)}) %all-to-all-start.1) | async-done | bytes 131104 | tf_op jit(solution)/shard_map/all_to_all | solution.py:93
  148.6 3.7 %collective-permute-start = (bf16[1,256,1024]{2,1,0:T(8,128)(2,1)S(1)}, bf16[1,256,1024]{2,1,0:T(8,128)(2,1)S(1)}, u32[]{:S(2)}, u32[]{:S(2)}) collective-permute-start(bf16[1,256,1024]{2,1,0:T(8,128)(2,1)S(1)} %bitcast.216), channel_id=1, source_target_pairs={{0,16},{1,17},{2,18},{3,19},{4,20},{5,21},{6,22},{7,23},{8,24},{9,... | collective-permute-start | bytes 1572872 | tf_op jit(solution)/shard_map/ppermute | solution.py:18
  152.4 9.5 %collective-permute-done = bf16[1,256,1024]{2,1,0:T(8,128)(2,1)S(1)} collective-permute-done((bf16[1,256,1024]{2,1,0:T(8,128)(2,1)S(1)}, bf16[1,256,1024]{2,1,0:T(8,128)(2,1)S(1)}, u32[]{:S(2)}, u32[]{:S(2)}) %collective-permute-start) | collective-permute-done | bytes 524320 | tf_op jit(solution)/shard_map/ppermute | solution.py:18
  162.5 1.1 fusion.17
  163.8 0.8 fusion.263
  164.7 1.1 convolution_convert_fusion
  165.9 0.5 convert_reduce_fusion.1
  167.1 0.9 convolution_convert_fusion.2
  167.9 3.9 %all-to-all-start.2 = ((bf16[1,4,16,1024]{3,2,0,1:T(8,128)(2,1)}), bf16[1,4,16,1024]{3,2,0,1:T(8,128)(2,1)S(1)}, u32[]{:S(2)}, u32[]{:S(2)}) async-start(bf16[1,4,16,1024]{3,2,0,1:T(8,128)(2,1)} %bitcast.48), calls=%async_computation.2 | async-start | bytes 262144 | tf_op jit(solution)/shard_map/all_to_all | solution.py:87
  172.1 5.7 %all-to-all-done.2 = bf16[1,4,16,1024]{3,2,0,1:T(8,128)(2,1)S(1)} async-done(((bf16[1,4,16,1024]{3,2,0,1:T(8,128)(2,1)}), bf16[1,4,16,1024]{3,2,0,1:T(8,128)(2,1)S(1)}, u32[]{:S(2)}, u32[]{:S(2)}) %all-to-all-start.2) | async-done | bytes 131104 | tf_op jit(solution)/shard_map/all_to_all | solution.py:87
  177.7 6.8 %fusion.37 = bf16[64,1024]{1,0:T(8,128)(2,1)} fusion(bf16[1,1,2048,1024]{3,2,1,0:T(8,128)(2,1)} %all-gather.13.cloned.1.call-done, bf16[64,1024]{1,0:T(8,128)(2,1)S(1)} %bitcast.225, bf16[1,1,1024,2048]{3,2,1,0:T(8,128)(2,1)} %all-gather.11.cloned.1.call-done), kind=kOutput, calls=%fused_computation.56 | convolution fusion | flops 545456128 | bytes 8650752 | tf_op jit(solution)/shard_map/dot_general | solution.py:92
  184.5 3.3 %all-to-all-start.3 = ((bf16[4,1,16,1024]{3,2,1,0:T(8,128)(2,1)}), bf16[4,1,16,1024]{3,2,1,0:T(8,128)(2,1)S(1)}, u32[]{:S(2)}, u32[]{:S(2)}) async-start(bf16[4,1,16,1024]{3,2,1,0:T(8,128)(2,1)} %bitcast.51), calls=%async_computation.3 | async-start | bytes 262144 | tf_op jit(solution)/shard_map/all_to_all | solution.py:93
  187.8 5.9 %all-to-all-done.3 = bf16[4,1,16,1024]{3,2,1,0:T(8,128)(2,1)S(1)} async-done(((bf16[4,1,16,1024]{3,2,1,0:T(8,128)(2,1)}), bf16[4,1,16,1024]{3,2,1,0:T(8,128)(2,1)S(1)}, u32[]{:S(2)}, u32[]{:S(2)}) %all-to-all-start.3) | async-done | bytes 131104 | tf_op jit(solution)/shard_map/all_to_all | solution.py:93
  194.1 1.1 maximum_bitcast_fusion
  (72 shorter events, 5.7 us)
Async XLA Ops:
  6.5 60.2 %copy-start = (bf16[1,1024,4]{1,2,0:T(4,128)(2,1)S(1)}, bf16[1,1024,4]{1,2,0:T(4,128)(2,1)}, u32[]{:S(2)}) copy-start(bf16[1,1024,4]{1,2,0:T(4,128)(2,1)} %param.17) | copy-start | bytes 24580
  6.5 2.8 %copy-start.4 = (s32[1,2,1,256,1]{3,4,2,1,0:T(1,128)S(1)}, s32[1,2,1,256,1]{3,4,2,1,0:T(1,128)}, u32[]{:S(2)}) copy-start(s32[1,2,1,256,1]{3,4,2,1,0:T(1,128)} %param.12) | copy-start | bytes 6148
  6.5 6.0 %copy-start.1 = (bf16[1,1,256,1024]{3,2,1,0:T(8,128)(2,1)S(1)}, bf16[1,1,256,1024]{3,2,1,0:T(8,128)(2,1)}, u32[]{:S(2)}) copy-start(bf16[1,1,256,1024]{3,2,1,0:T(8,128)(2,1)} %param.10) | copy-start | bytes 1572868
  6.5 33.7 %copy-start.7 = (f32[1,1024]{1,0:T(1,128)S(1)}, f32[1,1024]{1,0:T(1,128)}, u32[]{:S(2)}) copy-start(f32[1,1024]{1,0:T(1,128)} %param.13) | copy-start | bytes 12292
  6.5 33.7 %all-gather.7.cloned.1.call-start = ((), (), s32[]{:S(2)}) async-start(), calls=%async_computation.4 | async-start | bytes 3932160 | tf_op jit(solution)/shard_map/all_gather | solution.py:121
  7.3 51.2 %all-gather.9.cloned.1.call-start = ((), (), s32[]{:S(2)}) async-start(), calls=%async_computation.5 | async-start | bytes 1310720 | tf_op jit(solution)/shard_map/all_gather | solution.py:122
  8.0 86.6 %all-gather.11.cloned.1.call-start = ((), (), s32[]{:S(2)}) async-start(), calls=%async_computation.6 | async-start | bytes 5242880 | tf_op jit(solution)/shard_map/all_gather | solution.py:126
  8.8 121.8 %all-gather.13.cloned.1.call-start = ((), (), s32[]{:S(2)}) async-start(), calls=%async_computation.7 | async-start | bytes 5242880 | tf_op jit(solution)/shard_map/all_gather | solution.py:127
  45.4 15.2 %copy-start.3 = (f32[1,1024]{1,0:T(1,128)S(1)}, f32[1,1024]{1,0:T(1,128)}, u32[]{:S(2)}) copy-start(f32[1,1024]{1,0:T(1,128)} %param.16) | copy-start | bytes 12292
  61.9 10.9 %all-to-all-start = ((bf16[1,4,16,1024]{3,2,0,1:T(8,128)(2,1)}), bf16[1,4,16,1024]{3,2,0,1:T(8,128)(2,1)S(1)}, u32[]{:S(2)}, u32[]{:S(2)}) async-start(bf16[1,4,16,1024]{3,2,0,1:T(8,128)(2,1)} %bitcast.22), calls=%async_computation | async-start | bytes 262144 | tf_op jit(solution)/shard_map/all_to_all | solution.py:87
  130.5 31.4 %copy-start.2 = (bf16[1,256,1024]{2,1,0:T(8,128)(2,1)S(1)}, bf16[1,256,1024]{2,1,0:T(8,128)(2,1)}, u32[]{:S(2)}) copy-start(bf16[1,256,1024]{2,1,0:T(8,128)(2,1)} %param.11) | copy-start | bytes 1572868
  137.3 10.9 %all-to-all-start.1 = ((bf16[4,1,16,1024]{3,2,1,0:T(8,128)(2,1)}), bf16[4,1,16,1024]{3,2,1,0:T(8,128)(2,1)S(1)}, u32[]{:S(2)}, u32[]{:S(2)}) async-start(bf16[4,1,16,1024]{3,2,1,0:T(8,128)(2,1)} %bitcast.27), calls=%async_computation.1 | async-start | bytes 262144 | tf_op jit(solution)/shard_map/all_to_all | solution.py:93
  148.3 14.2 %copy-start.5 = (bf16[1,1024,1536]{2,1,0:T(8,128)(2,1)S(1)}, bf16[1,1024,1536]{2,1,0:T(8,128)(2,1)}, u32[]{:S(2)}) copy-start(bf16[1,1024,1536]{2,1,0:T(8,128)(2,1)} %all-gather.7.cloned.1.call-done) | copy-start | bytes 9437188
  148.6 13.3 %collective-permute-start = (bf16[1,256,1024]{2,1,0:T(8,128)(2,1)S(1)}, bf16[1,256,1024]{2,1,0:T(8,128)(2,1)S(1)}, u32[]{:S(2)}, u32[]{:S(2)}) collective-permute-start(bf16[1,256,1024]{2,1,0:T(8,128)(2,1)S(1)} %bitcast.216), channel_id=1, source_target_pairs={{0,16},{1,17},{2,18},{3,19},{4,20},{5,21},{6,22},{7,23},{8,24},{9,... | collective-permute-start | bytes 1572872 | tf_op jit(solution)/shard_map/ppermute | solution.py:18
  164.7 1.2 copy-start.6
  167.9 9.8 %all-to-all-start.2 = ((bf16[1,4,16,1024]{3,2,0,1:T(8,128)(2,1)}), bf16[1,4,16,1024]{3,2,0,1:T(8,128)(2,1)S(1)}, u32[]{:S(2)}, u32[]{:S(2)}) async-start(bf16[1,4,16,1024]{3,2,0,1:T(8,128)(2,1)} %bitcast.48), calls=%async_computation.2 | async-start | bytes 262144 | tf_op jit(solution)/shard_map/all_to_all | solution.py:87
  184.5 9.2 %all-to-all-start.3 = ((bf16[4,1,16,1024]{3,2,1,0:T(8,128)(2,1)}), bf16[4,1,16,1024]{3,2,1,0:T(8,128)(2,1)S(1)}, u32[]{:S(2)}, u32[]{:S(2)}) async-start(bf16[4,1,16,1024]{3,2,1,0:T(8,128)(2,1)} %bitcast.51), calls=%async_computation.3 | async-start | bytes 262144 | tf_op jit(solution)/shard_map/all_to_all | solution.py:93
Sparse Core Ops, SparseCore 0:
  8.9 31.2 all-gather.6
  41.8 16.7 all-gather.8
  60.1 34.4 all-gather.10
  96.0 34.4 all-gather.12
where the time goes:
time: 202 us
  waiting for transfers between devices  134 us (66%)
  matrix products  26.9 us (13%)
  starting transfers between devices  20.3 us (10%)
  between operations  13.3 us (7%)
  other arithmetic  5.87 us (3%)
    all_gather x1, waiting for transfers between devices, per_device(): lax.all_gather(expert_out[:, 0], 'dp', axis=1, tiled=True)  35.9 us
    all_gather x1, waiting for transfers between devices, per_device(): lax.all_gather(attention_in, 'dp', axis=1, tiled=True)  27.2 us
    all_gather x1, waiting for transfers between devices, per_device(): lax.all_gather(expert_in[:, 0], 'dp', axis=1, tiled=True)  21.8 us
    dot_general x2, matrix products, route_and_mix(): jnp.dot(hidden, own_out, preferred_element_type=jnp.float32)  13.6 us
    all_gather x1, waiting for transfers between devices, per_device(): lax.all_gather(attention_out, 'dp', axis=1, tiled=True)  13.1 us
    all_to_all x2, waiting for transfers between devices, route_and_mix(): lax.all_to_all(answer.reshape(arrived.shape), 'expert', split_axis=0, con...  12.2 us
    all_to_all x2, waiting for transfers between devices, route_and_mix(): lax.all_to_all(outgoing, 'expert', split_axis=1, concat_axis=0, tiled=True)  11.5 us
    ppermute x1, waiting for transfers between devices, shifted(): return lax.ppermute(shard, axis, pairs)  9.51 us
  transfers between devices with their start and end apart: 9, of which 9 were waited for; matrix products, arithmetic and copies ran while one was open for 6% of the time, Pallas kernels for 0%

commit v1 on v0

v1 whole, which is shorter than its diff:
```python
import functools

import jax
import jax.numpy as jnp
from jax import lax
from jax.experimental import pallas as pl
from jax.experimental.pallas import tpu as pltpu
from jax.sharding import PartitionSpec as P

HEAD_DIM = 64
CAP = 16
EPSILON = 1e-06
MESH = pl.DeviceIdType.MESH
F32, BF16 = jnp.float32, jnp.bfloat16
LANES = 128


def dot(a, b):
    return jnp.dot(a, b, preferred_element_type=F32)


def rows_of(start, size):
    return pl.ds(pl.multiple_of(start, 16), size)


def kernel(
    dp, ex, pieces,
    inbound, queued, routes, gain_a, att_in, att_out, gain_b, router, exp_in, exp_out,
    out,
    full_in, full_out, w1, normed, qkv, ctx, entering, mixed, table, table_t, onehot, gate, sent,
    rows, partial, parts, answer, answered, far_mixed, far_gate, far_ans, hid,
    own_sem, sib_s, sib_r, y_s, y_r, fz_s, fz_r, fs_s, fs_r, gs_s, gs_r, w_s, w_r,
    z1_s, z1_r, g_s, g_r, p_s, p_r, z2_s, z2_r, x_s, x_r,
):
    sec, d, e = lax.axis_index("section"), lax.axis_index("dp"), lax.axis_index("expert")
    y, c, half = d // 2, d % 2, e % 2
    ny = dp // 2
    sib, zpal, far = y * 2 + 1 - c, e + 1 - 2 * half, 1 - sec
    seq, width = inbound.shape
    k_rows = ex * CAP
    hid_own = w1.shape[1]
    heads_w = full_out.shape[0]
    in_rows, out_rows = att_in.shape[0], att_out.shape[0]

    def copy(src, dst, s_sem, r_sem, to):
        return pltpu.make_async_remote_copy(
            src_ref=src, dst_ref=dst, send_sem=s_sem, recv_sem=r_sem,
            device_id=to, device_id_type=MESH,
        )

    barrier = pltpu.get_barrier_semaphore()
    for k in range(1, dp):
        pl.semaphore_signal(barrier, inc=1, device_id={"dp": lax.rem(d + k, dp)}, device_id_type=MESH)
    for k in range(1, ex):
        pl.semaphore_signal(barrier, inc=1, device_id={"expert": lax.rem(e + k, ex)}, device_id_type=MESH)
    pl.semaphore_signal(barrier, inc=1, device_id={"section": far}, device_id_type=MESH)
    pl.semaphore_wait(barrier, dp + ex - 1)

    pending = []

    def send(*a):
        one = copy(*a)
        one.start()
        pending.append(one)

    leaving = []

    def leave(*a):
        one = copy(*a)
        one.start()
        leaving.append(one)

    weights = ((0, att_in, full_in, in_rows, pieces[0]), (1, att_out, full_out, out_rows, pieces[1]))
    chunk_list = []
    base = 0
    for which, src, dst, n, cuts in weights:
        size = n // 2 // cuts
        for i in range(cuts):
            chunk_list.append((base + i, src, dst, n, size, i))
        base += cuts
    for idx, src, dst, n, size, i in chunk_list:
        for k in range(1, ny):
            there = lax.rem(y + k, ny) * 2 + c
            off = half * (n // 2) + i * size
            send(src.at[rows_of(off, size)], dst.at[rows_of(d * n + off, size)],
                 y_s.at[idx, k - 1], y_r.at[idx, k - 1], {"dp": there})
    own = []
    for which, src, dst, n, cuts in weights:
        send(src, dst.at[rows_of(d * n, n)], sib_s.at[which], sib_r.at[which], {"dp": sib})
        here = pltpu.make_async_copy(src, dst.at[rows_of(d * n, n)], own_sem.at[which])
        here.start()
        own.append(here)
    w_rows = exp_in.shape[0]
    here = pltpu.make_async_copy(
        exp_in.at[:, pl.ds(pl.multiple_of(d * hid_own, LANES), hid_own)],
        w1.at[rows_of(d * w_rows, w_rows)], own_sem.at[2])
    here.start()
    own.append(here)

    lane = lax.broadcasted_iota(jnp.int32, (seq, LANES), 1)
    wide = table_t.shape[1]
    slots = lax.broadcasted_iota(jnp.int32, (seq, wide), 1)
    earlier = (lax.broadcasted_iota(jnp.int32, (seq, seq), 0)
               > lax.broadcasted_iota(jnp.int32, (seq, seq), 1)).astype(F32).astype(BF16)
    slot_of = []
    for t in range(2):
        chosen = routes[t]
        hot = (lane == chosen).astype(F32)
        place = jnp.sum(dot(earlier, hot.astype(BF16)) * hot, axis=1, keepdims=True)
        slot = jnp.where(place < CAP, chosen.astype(F32) * CAP + place, -1.0)
        full = (slots.astype(F32) == slot).astype(F32)
        table[t] = full[:, :k_rows].astype(BF16)
        table_t[t] = full.T.astype(BF16)
        onehot[t] = hot
        slot_of.append(slot)

    def norm(src, gain):
        step = 32

        def body(i, _):
            at = pl.ds(pl.multiple_of(i * step, step), step)
            v = src[at, :].astype(F32)
            centre = v - jnp.mean(v, axis=-1, keepdims=True)
            spread = jnp.mean(centre * centre, axis=-1, keepdims=True)
            normed[at, :] = (centre * lax.rsqrt(spread + EPSILON) * gain[...]).astype(BF16)
            return 0

        lax.fori_loop(0, seq // step, body, 0)

    norm(inbound, gain_a)

    for idx, src, dst, n, size, i in chunk_list:
        for k in range(1, ny):
            come = lax.rem(y - k + ny, ny) * 2 + c
            view = dst.at[rows_of(come * n + half * (n // 2) + i * size, size)]
            copy(view, view, y_s.at[idx, k - 1], y_r.at[idx, k - 1], {"dp": come}).wait_recv()
            send(view, view, fz_s.at[idx, k - 1], fz_r.at[idx, k - 1], {"expert": zpal})
            send(view, view, fs_s.at[idx, k - 1], fs_r.at[idx, k - 1], {"dp": sib})
    for k in range(1, dp):
        to = lax.rem(d + k, dp)
        send(exp_in.at[:, pl.ds(pl.multiple_of(to * hid_own, LANES), hid_own)],
             w1.at[rows_of(d * w_rows, w_rows)], w_s.at[k - 1], w_r.at[k - 1], {"dp": to})
    for idx, src, dst, n, size, i in chunk_list:
        for k in range(1, ny):
            come = lax.rem(y - k + ny, ny) * 2 + c
            view = dst.at[rows_of(come * n + (1 - half) * (n // 2) + i * size, size)]
            copy(view, view, fz_s.at[idx, k - 1], fz_r.at[idx, k - 1], {"expert": zpal}).wait_recv()
            send(view, view, gs_s.at[idx, k - 1], gs_r.at[idx, k - 1], {"dp": sib})

    def land(which):
        _, src, dst, n, cuts = weights[which]
        own[which].wait()
        view = dst.at[rows_of(sib * n, n)]
        copy(view, view, sib_s.at[which], sib_r.at[which], {"dp": sib}).wait_recv()
        for idx, _, to, n, size, i in chunk_list:
            if to is not dst:
                continue
            for k in range(1, ny):
                come = lax.rem(y - k + ny, ny) * 2 + 1 - c
                view = dst.at[rows_of(come * n + half * (n // 2) + i * size, size)]
                copy(view, view, fs_s.at[idx, k - 1], fs_r.at[idx, k - 1], {"dp": sib}).wait_recv()
                view = dst.at[rows_of(come * n + (1 - half) * (n // 2) + i * size, size)]
                copy(view, view, gs_s.at[idx, k - 1], gs_r.at[idx, k - 1], {"dp": sib}).wait_recv()

    low = lax.broadcasted_iota(jnp.int32, (seq, LANES), 1) < HEAD_DIM

    for t in range(2):
        if t == 0:
            source = inbound
            land(0)
        else:
            source = entering
            for i, view in enumerate((far_mixed, far_gate, far_ans)):
                copy(view, view, x_s.at[i], x_r.at[i], {"section": far}).wait_recv()
            far_table = (slots.astype(F32) == far_gate[:, 1:2]).astype(F32)[:, :k_rows].astype(BF16)
            for j in range(0, width, 256):
                at = slice(j, j + 256)
                came = (far_mixed[:, at].astype(F32)
                        + far_gate[:, 0:1] * dot(far_table, far_ans[:, at]))
                entering[:, at] = jnp.where(sec == 0, queued[:, at].astype(F32), came).astype(BF16)
            norm(entering, gain_a)
        for j in range(0, 3 * heads_w, 256):
            qkv[:, j:j + 256] = dot(normed[...], full_in[:, j:j + 256]).astype(BF16)
        for j in range(0, heads_w, LANES):
            q = qkv[:, j:j + LANES] * jnp.asarray(HEAD_DIM ** -0.5, BF16)
            key = qkv[:, heads_w + j:heads_w + j + LANES]
            val = qkv[:, 2 * heads_w + j:2 * heads_w + j + LANES]
            both = []
            for mask in (low, jnp.logical_not(low)):
                one = jnp.where(mask, q.astype(F32), 0.0).astype(BF16)
                s = lax.dot_general(one, key, (((1,), (1,)), ((), ())), preferred_element_type=F32)
                w = jnp.exp(s - jnp.max(s, axis=1, keepdims=True))
                both.append(dot(w.astype(BF16), val) / jnp.sum(w, axis=1, keepdims=True))
            ctx[:, j:j + LANES] = jnp.where(low, both[0], both[1]).astype(BF16)
        if t == 0:
            land(1)
        for j in range(0, width, 256):
            at = slice(j, j + 256)
            mixed[t, :, at] = (source[:, at].astype(F32) + dot(ctx[...], full_out[:, at])).astype(BF16)
        if t == 0:
            send(mixed.at[0], far_mixed, x_s.at[0], x_r.at[0], {"section": far})
        norm(mixed.at[t], gain_b)
        for j in range(0, width, 256):
            at = slice(j, j + 256)
            sent[t, :, at] = dot(table_t[t], normed[:, at])[:].astype(BF16)
        for k in range(1, ex):
            to = lax.rem(e + k, ex)
            send(sent.at[t, rows_of(to * CAP, CAP)], rows.at[t, d, rows_of(e * CAP, CAP)],
                 z1_s.at[t, k - 1], z1_r.at[t, k - 1], {"expert": to})
        rows[t, d, rows_of(e * CAP, CAP), :] = sent[t, rows_of(e * CAP, CAP), :]
        logits = dot(normed[...], router[...])
        picked = jnp.sum(logits * onehot[t][:, :ex], axis=1, keepdims=True)
        gating = 1.0 / (1.0 + jnp.exp(-picked))
        gate[t] = jnp.where(lane == 0, gating, jnp.where(lane == 1, slot_of[t], 0.0))
        if t == 0:
            send(gate.at[0], far_gate, x_s.at[1], x_r.at[1], {"section": far})
        for k in range(1, ex):
            come = lax.rem(e - k + ex, ex)
            view = rows.at[t, d, rows_of(come * CAP, CAP)]
            copy(view, view, z1_s.at[t, k - 1], z1_r.at[t, k - 1], {"expert": come}).wait_recv()
        for k in range(1, dp):
            send(rows.at[t, d], rows.at[t, d], g_s.at[t, k - 1], g_r.at[t, k - 1],
                 {"dp": lax.rem(d + k, dp)})
        if t == 0:
            own[2].wait()
            for k in range(1, dp):
                come = lax.rem(d - k + dp, dp)
                view = w1.at[rows_of(come * w_rows, w_rows)]
                copy(view, view, w_s.at[k - 1], w_r.at[k - 1], {"dp": come}).wait_recv()
        for k in range(1, dp):
            come = lax.rem(d - k + dp, dp)
            view = rows.at[t, come]
            copy(view, view, g_s.at[t, k - 1], g_r.at[t, k - 1], {"dp": come}).wait_recv()

        group = 4

        def experts(i, _):
            at = pl.ds(i * group, group)
            x = rows[t, at].reshape(group * k_rows, width)
            for j in range(0, hid_own, 128):
                h = dot(x, w1[:, j:j + 128])
                h = 0.5 * h * (1.0 + lax.erf(h * 0.7071067811865476))
                hid[:, j:j + 128] = h.astype(BF16)
            for j in range(0, width, 256):
                a = dot(hid[...], exp_out[:, j:j + 256]).astype(BF16)
                partial[at, :, j:j + 256] = a.reshape(group, k_rows, 256)
            return 0

        for one in leaving:
            one.wait_send()
        leaving.clear()
        lax.fori_loop(0, dp // group, experts, 0)
        for k in range(1, dp):
            to = lax.rem(d + k, dp)
            leave(partial.at[to], parts.at[t, k - 1], p_s.at[t, k - 1], p_r.at[t, k - 1], {"dp": to})
        for k in range(1, dp):
            come = lax.rem(d - k + dp, dp)
            view = parts.at[t, k - 1]
            copy(view, view, p_s.at[t, k - 1], p_r.at[t, k - 1], {"dp": come}).wait_recv()
        for i in range(ex):
            at = slice(i * CAP, i * CAP + CAP)
            total = partial[d, at, :].astype(F32)
            for k in range(1, dp):
                total += parts[t, k - 1, at, :].astype(F32)
            answer[t, at, :] = total.astype(BF16)
        for k in range(1, ex):
            to = lax.rem(e + k, ex)
            send(answer.at[t, rows_of(to * CAP, CAP)], answered.at[t, rows_of(e * CAP, CAP)],
                 z2_s.at[t, k - 1], z2_r.at[t, k - 1], {"expert": to})
        answered[t, rows_of(e * CAP, CAP), :] = answer[t, rows_of(e * CAP, CAP), :]
        for k in range(1, ex):
            come = lax.rem(e - k + ex, ex)
            view = answered.at[t, rows_of(come * CAP, CAP)]
            copy(view, view, z2_s.at[t, k - 1], z2_r.at[t, k - 1], {"expert": come}).wait_recv()
        if t == 0:
            send(answered.at[0], far_ans, x_s.at[2], x_r.at[2], {"section": far})
        for j in range(0, width, 256):
            at = slice(j, j + 256)
            out[t, :, at] = (mixed[t, :, at].astype(F32)
                             + gate[t][:, 0:1] * dot(table[t], answered[t, :, at])).astype(BF16)
    for one in pending + leaving:
        one.wait_send()


def per_device(dp, ex, inbound, queued, routes, gain_a, att_in, att_out, gain_b, router, exp_in, exp_out):
    seq, width = queued.shape[1:]
    k_rows = ex * CAP
    wide = max(k_rows, LANES)
    hid_own = exp_out.shape[2]
    heads_w = att_out.shape[1] * dp
    cols = att_in.shape[2]
    in_rows, out_rows = att_in.shape[1], att_out.shape[1]
    pieces = (max(1, min(4, in_rows // 32)), max(1, min(2, out_rows // 32)))
    n, ny = sum(pieces), max(dp // 2 - 1, 1)
    vm, dma = pltpu.VMEM, pltpu.SemaphoreType.DMA
    scratch = [
        vm((width, cols), BF16), vm((heads_w, width), BF16), vm((width, hid_own), BF16),
        vm((seq, width), BF16), vm((seq, cols), BF16), vm((seq, heads_w), BF16),
        vm((seq, width), BF16), vm((2, seq, width), BF16), vm((2, seq, k_rows), BF16),
        vm((2, wide, seq), BF16), vm((2, seq, LANES), F32), vm((2, seq, LANES), F32),
        vm((2, wide, width), BF16),
        vm((2, dp, k_rows, width), BF16), vm((dp, k_rows, width), BF16),
        vm((2, dp - 1, k_rows, width), BF16),
        vm((2, k_rows, width), BF16), vm((2, k_rows, width), BF16),
        vm((seq, width), BF16), vm((seq, LANES), F32), vm((k_rows, width), BF16),
        vm((4 * k_rows, hid_own), BF16),
        dma((3,)), dma((2,)), dma((2,)),
        *[dma((n, ny))] * 8,
        dma((dp - 1,)), dma((dp - 1,)),
        dma((2, ex - 1)), dma((2, ex - 1)), dma((2, dp - 1)), dma((2, dp - 1)),
        dma((2, dp - 1)), dma((2, dp - 1)), dma((2, ex - 1)), dma((2, ex - 1)),
        dma((3,)), dma((3,)),
    ]
    result = pl.pallas_call(
        functools.partial(kernel, dp, ex, pieces),
        out_shape=jax.ShapeDtypeStruct((2, seq, width), BF16),
        in_specs=[pl.BlockSpec(memory_space=pltpu.VMEM)] * 10,
        out_specs=pl.BlockSpec(memory_space=pltpu.VMEM),
        scratch_shapes=scratch,
        compiler_params=pltpu.CompilerParams(
            collective_id=0, has_side_effects=True, vmem_limit_bytes=60 * 2**20
        ),
    )(
        inbound[0, 0], queued[0], routes[0, :, 0], gain_a, att_in[0], att_out[0], gain_b,
        router[0], exp_in[0, 0], exp_out[0, 0],
    )
    return result[None, :, None]


def solution(mesh):
    in_specs = (
        P("section", ("dp", "expert"), None, None),
        P(("dp", "expert"), None, None),
        P("section", None, ("dp", "expert"), None, None),
        P("section", None),
        P("section", "dp", None),
        P("section", "dp", None),
        P("section", None),
        P("section", None, None),
        P("section", "expert", "dp", None),
        P("section", "expert", "dp", None),
    )
    out_specs = P("section", None, ("dp", "expert"), None, None)
    return jax.shard_map(
        functools.partial(per_device, mesh.shape["dp"], mesh.shape["expert"]),
        mesh=mesh, in_specs=in_specs, out_specs=out_specs, check_vma=False,
    )
```

time: 202 us -> 90.8 us (0.45)
  waiting for transfers between devices: 134 us -> 0 us
  Pallas kernels: 0 us -> 85.2 us
  matrix products: 26.9 us -> 0 us
  starting transfers between devices: 20.3 us -> 0 us
  between operations: 13.3 us -> 0.02 us
  other arithmetic: 5.87 us -> 0.02 us
  local copies, waits for them, and re-layouts: 1.49 us -> 4.68 us
    all_gather x4 -> x0, waiting for transfers between devices: 98.1 us -> none  [the longest x1 35.9 us: per_device(): lax.all_gather(expert_out[:, 0], 'dp', axis=1, tiled=True)]
    pallas_call x0 -> x1, Pallas kernels: none -> 85.2 us  [per_device(): pl.pallas_call(functools.partial(kernel, dp, ex, pieces), out_shape=jax.S...]
    dot_general x14 -> x0, matrix products: 25.2 us -> none  [the longest x2 13.6 us: route_and_mix(): jnp.dot(hidden, own_out, preferred_element_type=jnp.float32)]
    all_to_all x4 -> x0, waiting for transfers between devices: 23.7 us -> none  [the longest x2 12.2 us: route_and_mix(): lax.all_to_all(answer.reshape(arrived.shape), 'expert', split_axis=0, con...]
    all_to_all x4 -> x0, starting transfers between devices: 16.4 us -> none  [the longest x2 8.48 us: route_and_mix(): lax.all_to_all(outgoing, 'expert', split_axis=1, concat_axis=0, tiled=True)]
    ppermute x1 -> x0, waiting for transfers between devices: 9.51 us -> none  [shifted(): return lax.ppermute(shard, axis, pairs)]
    ppermute x1 -> x0, starting transfers between devices: 3.72 us -> none  [shifted(): return lax.ppermute(shard, axis, pairs)]
    unnamed x16 -> x6, local copies, waits for them, and re-layouts: 0.15 us -> 3.84 us
  transfers between devices with their start and end apart: 9 -> 0, of which waited for: 9 -> 0; matrix products, arithmetic and copies ran while one was open for 6% -> 0% of each run, Pallas kernels for 0% -> 0%
where the time goes in v1:
time: 90.8 us; the launch traced here: 89.9 us
  Pallas kernels  85.2 us (94%)
  local copies, waits for them, and re-layouts  4.68 us (5%)
    pallas_call x1, Pallas kernels, per_device(): pl.pallas_call(functools.partial(kernel, dp, ex, pieces), out_shape=jax.S...  85.2 us
    unnamed x6, local copies, waits for them, and re-layouts  3.84 us

profile of v1, /device:TPU:0, one launch (start us, length us, event | category | flops | bytes accessed | tf_op | source)
XLA Modules:
  0.0 89.9 jit_solution(11652944661290071265)
XLA Ops:
  0.0 0.0 copy-start.1
  0.0 0.7 copy-done.1
  0.7 0.0 copy-start
  0.7 0.8 squeeze.32.routes
  1.5 0.0 copy-done
  1.5 0.9 copy.13
  2.4 85.2 %shard_map.100 = bf16[2,256,1024]{2,1,0:T(8,128)(2,1)} custom-call(bf16[256,1024]{1,0:T(8,128)(2,1)} %bitcast.15, bf16[256,1024]{1,0:T(8,128)(2,1)} %bitcast.16, s32[2,256,1]{2,1,0:T(8,128)} %squeeze.32.routes, f32[1,1024]{1,0:T(1,128)} %gain_a.1, bf16[256,1536]{1,0:T(8,128)(2,1)} %bitcast.14, bf16[128,1024]{1,0:T(8,128)(2,1)} %bitcast.17, ...), custom_call_target="tpu_custom_call" | custom-call | tf_op jit(solution)/shard_map/pallas_call | solution.py:314
  87.7 2.3 %copy.17 = bf16[1,2,1,256,1024]{4,3,2,1,0:T(8,128)(2,1)} copy(bf16[1,2,1,256,1024]{4,3,2,1,0:T(8,128)(2,1)} %bitcast.10) | data formatting | bytes 2097152
  (1 shorter events, 0.0 us)
Async XLA Ops:
  0.0 0.7 copy-start.1
  0.7 0.8 copy-start

commit v2 on v1

--- a/solution.py
+++ b/solution.py
@@ -25,12 +25,13 @@
 
 def kernel(
     dp, ex, pieces,
-    inbound, queued, routes, gain_a, att_in, att_out, gain_b, router, exp_in, exp_out,
-    out,
+    inbound_h, queued_h, routes, gain_a, att_in, att_out, gain_b, router, exp_in, exp_out_h,
+    out_h,
+    inbound, queued, exp_out, out,
     full_in, full_out, w1, normed, qkv, ctx, entering, mixed, table, table_t, onehot, gate, sent,
-    rows, partial, parts, answer, answered, far_mixed, far_gate, far_ans, hid,
-    own_sem, sib_s, sib_r, y_s, y_r, fz_s, fz_r, fs_s, fs_r, gs_s, gs_r, w_s, w_r,
-    z1_s, z1_r, g_s, g_r, p_s, p_r, z2_s, z2_r, x_s, x_r,
+    rows, partial, near, parts, answer, answered, far_mixed, far_gate, far_ans, hid,
+    own_sem, load_sem, save_sem, sib_s, sib_r, y_s, y_r, fz_s, fz_r, fs_s, fs_r, gs_s, gs_r, w_s, w_r,
+    z1_s, z1_r, g_s, g_r, h_s, h_r, n_s, n_r, p_s, p_r, z2_s, z2_r, x_s, x_r,
 ):
     sec, d, e = lax.axis_index("section"), lax.axis_index("dp"), lax.axis_index("expert")
     y, c, half = d // 2, d % 2, e % 2
@@ -48,6 +49,10 @@
             device_id=to, device_id_type=MESH,
         )
 
+    loads = []
+    for i, (a, b) in enumerate(((inbound_h, inbound), (queued_h, queued), (exp_out_h, exp_out))):
+        loads.append(pltpu.make_async_copy(a, b, load_sem.at[i]))
+    loads[0].start()
     barrier = pltpu.get_barrier_semaphore()
     for k in range(1, dp):
         pl.semaphore_signal(barrier, inc=1, device_id={"dp": lax.rem(d + k, dp)}, device_id_type=MESH)
@@ -97,6 +102,9 @@
     here.start()
     own.append(here)
 
+    loads[1].start()
+    loads[2].start()
+
     lane = lax.broadcasted_iota(jnp.int32, (seq, LANES), 1)
     wide = table_t.shape[1]
     slots = lax.broadcasted_iota(jnp.int32, (seq, wide), 1)
@@ -104,10 +112,10 @@
                > lax.broadcasted_iota(jnp.int32, (seq, seq), 1)).astype(F32).astype(BF16)
     slot_of = []
     for t in range(2):
-        chosen = routes[t]
-        hot = (lane == chosen).astype(F32)
+        chosen = jnp.broadcast_to(routes[t:t + 1, :].astype(F32), (LANES, seq)).T
+        hot = (lane.astype(F32) == chosen).astype(F32)
         place = jnp.sum(dot(earlier, hot.astype(BF16)) * hot, axis=1, keepdims=True)
-        slot = jnp.where(place < CAP, chosen.astype(F32) * CAP + place, -1.0)
+        slot = jnp.where(place < CAP, chosen[:, :1] * CAP + place, -1.0)
         full = (slots.astype(F32) == slot).astype(F32)
         table[t] = full[:, :k_rows].astype(BF16)
         table_t[t] = full.T.astype(BF16)
@@ -125,8 +133,9 @@
             normed[at, :] = (centre * lax.rsqrt(spread + EPSILON) * gain[...]).astype(BF16)
             return 0
 
-        lax.fori_loop(0, seq // step, body, 0)
-
+        lax.fori_loop(0, seq // step, body, 0, unroll=True)
+
+    loads[0].wait()
     norm(inbound, gain_a)
 
     for idx, src, dst, n, size, i in chunk_list:
@@ -162,15 +171,20 @@
                 view = dst.at[rows_of(come * n + (1 - half) * (n // 2) + i * size, size)]
                 copy(view, view, gs_s.at[idx, k - 1], gs_r.at[idx, k - 1], {"dp": sib}).wait_recv()
 
+    far_views = [far_mixed, far_gate]
+    for k in range(ex):
+        far_views.append(far_ans.at[rows_of(lax.rem(e - k + ex, ex) * CAP, CAP)])
     low = lax.broadcasted_iota(jnp.int32, (seq, LANES), 1) < HEAD_DIM
 
+    saves = []
     for t in range(2):
         if t == 0:
             source = inbound
             land(0)
         else:
             source = entering
-            for i, view in enumerate((far_mixed, far_gate, far_ans)):
+            loads[1].wait()
+            for i, view in enumerate(far_views):
                 copy(view, view, x_s.at[i], x_r.at[i], {"section": far}).wait_recv()
             far_table = (slots.astype(F32) == far_gate[:, 1:2]).astype(F32)[:, :k_rows].astype(BF16)
             for j in range(0, width, 256):
@@ -208,29 +222,44 @@
             send(sent.at[t, rows_of(to * CAP, CAP)], rows.at[t, d, rows_of(e * CAP, CAP)],
                  z1_s.at[t, k - 1], z1_r.at[t, k - 1], {"expert": to})
         rows[t, d, rows_of(e * CAP, CAP), :] = sent[t, rows_of(e * CAP, CAP), :]
-        logits = dot(normed[...], router[...])
+        logits = lax.dot_general(normed[...], router[...], (((1,), (1,)), ((), ())), preferred_element_type=F32)
         picked = jnp.sum(logits * onehot[t][:, :ex], axis=1, keepdims=True)
         gating = 1.0 / (1.0 + jnp.exp(-picked))
         gate[t] = jnp.where(lane == 0, gating, jnp.where(lane == 1, slot_of[t], 0.0))
         if t == 0:
             send(gate.at[0], far_gate, x_s.at[1], x_r.at[1], {"section": far})
-        for k in range(1, ex):
-            come = lax.rem(e - k + ex, ex)
+        def pass_on(kk):
+            at = rows_of(lax.rem(e - kk + ex, ex) * CAP, CAP)
+            for k in range(1, ny):
+                come = lax.rem(y - k + ny, ny) * 2 + c
+                view = rows.at[t, come, at]
+                copy(view, view, g_s.at[t, kk, k - 1], g_r.at[t, kk, k - 1], {"dp": come}).wait_recv()
+                send(view, view, h_s.at[t, kk, k], h_r.at[t, kk, k], {"dp": sib})
+
+        for kk in range(ex):
+            come = lax.rem(e - kk + ex, ex)
             view = rows.at[t, d, rows_of(come * CAP, CAP)]
-            copy(view, view, z1_s.at[t, k - 1], z1_r.at[t, k - 1], {"expert": come}).wait_recv()
-        for k in range(1, dp):
-            send(rows.at[t, d], rows.at[t, d], g_s.at[t, k - 1], g_r.at[t, k - 1],
-                 {"dp": lax.rem(d + k, dp)})
+            if kk > 0:
+                copy(view, view, z1_s.at[t, kk - 1], z1_r.at[t, kk - 1], {"expert": come}).wait_recv()
+            for k in range(1, ny):
+                send(view, view, g_s.at[t, kk, k - 1], g_r.at[t, kk, k - 1],
+                     {"dp": lax.rem(y + k, ny) * 2 + c})
+            send(view, view, h_s.at[t, kk, 0], h_r.at[t, kk, 0], {"dp": sib})
+            if kk > 0:
+                pass_on(kk - 1)
+        pass_on(ex - 1)
         if t == 0:
             own[2].wait()
+            loads[2].wait()
             for k in range(1, dp):
                 come = lax.rem(d - k + dp, dp)
                 view = w1.at[rows_of(come * w_rows, w_rows)]
                 copy(view, view, w_s.at[k - 1], w_r.at[k - 1], {"dp": come}).wait_recv()
-        for k in range(1, dp):
-            come = lax.rem(d - k + dp, dp)
-            view = rows.at[t, come]
-            copy(view, view, g_s.at[t, k - 1], g_r.at[t, k - 1], {"dp": come}).wait_recv()
+        for kk in range(ex):
+            at = rows_of(lax.rem(e - kk + ex, ex) * CAP, CAP)
+            for k in range(ny):
+                view = rows.at[t, lax.rem(y - k + ny, ny) * 2 + 1 - c, at]
+                copy(view, view, h_s.at[t, kk, k], h_r.at[t, kk, k], {"dp": sib}).wait_recv()
 
         group = 4
 
@@ -250,34 +279,51 @@
             one.wait_send()
         leaving.clear()
         lax.fori_loop(0, dp // group, experts, 0)
-        for k in range(1, dp):
-            to = lax.rem(d + k, dp)
-            leave(partial.at[to], parts.at[t, k - 1], p_s.at[t, k - 1], p_r.at[t, k - 1], {"dp": to})
-        for k in range(1, dp):
-            come = lax.rem(d - k + dp, dp)
-            view = parts.at[t, k - 1]
-            copy(view, view, p_s.at[t, k - 1], p_r.at[t, k - 1], {"dp": come}).wait_recv()
-        for i in range(ex):
-            at = slice(i * CAP, i * CAP + CAP)
-            total = partial[d, at, :].astype(F32)
-            for k in range(1, dp):
+        for k in (*range(1, ny), 0):
+            to = lax.rem(y + k, ny) * 2
+            leave(partial.at[to + 1 - c], near.at[t, k], n_s.at[t, k], n_r.at[t, k], {"dp": sib})
+        for k in range(1, ny):
+            to = lax.rem(y + k, ny) * 2 + c
+            view = near.at[t, k]
+            copy(view, view, n_s.at[t, k], n_r.at[t, k], {"dp": sib}).wait_recv()
+            for kk in (*range(1, ex), 0):
+                at = rows_of(lax.rem(e + kk, ex) * CAP, CAP)
+                partial[to, at, :] = (partial[to, at, :].astype(F32) + near[t, k, at, :].astype(F32)).astype(BF16)
+                leave(partial.at[to, at], parts.at[t, k - 1, at],
+                      p_s.at[t, kk, k - 1], p_r.at[t, kk, k - 1], {"dp": to})
+        view = near.at[t, 0]
+        copy(view, view, n_s.at[t, 0], n_r.at[t, 0], {"dp": sib}).wait_recv()
+        for kk in (*range(1, ex), 0):
+            to = lax.rem(e + kk, ex)
+            at = rows_of(to * CAP, CAP)
+            total = partial[d, at, :].astype(F32) + near[t, 0, at, :].astype(F32)
+            for k in range(1, ny):
+                view = parts.at[t, k - 1, at]
+                copy(view, view, p_s.at[t, kk, k - 1], p_r.at[t, kk, k - 1],
+                     {"dp": lax.rem(y - k + ny, ny) * 2 + c}).wait_recv()
                 total += parts[t, k - 1, at, :].astype(F32)
-            answer[t, at, :] = total.astype(BF16)
-        for k in range(1, ex):
-            to = lax.rem(e + k, ex)
-            send(answer.at[t, rows_of(to * CAP, CAP)], answered.at[t, rows_of(e * CAP, CAP)],
-                 z2_s.at[t, k - 1], z2_r.at[t, k - 1], {"expert": to})
-        answered[t, rows_of(e * CAP, CAP), :] = answer[t, rows_of(e * CAP, CAP), :]
-        for k in range(1, ex):
-            come = lax.rem(e - k + ex, ex)
+            if kk > 0:
+                answer[t, at, :] = total.astype(BF16)
+                send(answer.at[t, at], answered.at[t, rows_of(e * CAP, CAP)],
+                     z2_s.at[t, kk - 1], z2_r.at[t, kk - 1], {"expert": to})
+            else:
+                answered[t, at, :] = total.astype(BF16)
+        for kk in range(ex):
+            come = lax.rem(e - kk + ex, ex)
             view = answered.at[t, rows_of(come * CAP, CAP)]
-            copy(view, view, z2_s.at[t, k - 1], z2_r.at[t, k - 1], {"expert": come}).wait_recv()
-        if t == 0:
-            send(answered.at[0], far_ans, x_s.at[2], x_r.at[2], {"section": far})
+            if kk > 0:
+                copy(view, view, z2_s.at[t, kk - 1], z2_r.at[t, kk - 1], {"expert": come}).wait_recv()
+            if t == 0:
+                send(view, far_views[2 + kk], x_s.at[2 + kk], x_r.at[2 + kk], {"section": far})
         for j in range(0, width, 256):
             at = slice(j, j + 256)
             out[t, :, at] = (mixed[t, :, at].astype(F32)
                              + gate[t][:, 0:1] * dot(table[t], answered[t, :, at])).astype(BF16)
+        saving = pltpu.make_async_copy(out.at[t], out_h.at[t], save_sem.at[t])
+        saving.start()
+        saves.append(saving)
+    for one in saves:
+        one.wait()
     for one in pending + leaving:
         one.wait_send()
 
@@ -293,36 +339,40 @@
     pieces = (max(1, min(4, in_rows // 32)), max(1, min(2, out_rows // 32)))
     n, ny = sum(pieces), max(dp // 2 - 1, 1)
     vm, dma = pltpu.VMEM, pltpu.SemaphoreType.DMA
+    dev = dp // 2
     scratch = [
+        vm((seq, width), BF16), vm((seq, width), BF16), vm((hid_own, width), BF16), vm((2, seq, width), BF16),
         vm((width, cols), BF16), vm((heads_w, width), BF16), vm((width, hid_own), BF16),
         vm((seq, width), BF16), vm((seq, cols), BF16), vm((seq, heads_w), BF16),
         vm((seq, width), BF16), vm((2, seq, width), BF16), vm((2, seq, k_rows), BF16),
         vm((2, wide, seq), BF16), vm((2, seq, LANES), F32), vm((2, seq, LANES), F32),
         vm((2, wide, width), BF16),
         vm((2, dp, k_rows, width), BF16), vm((dp, k_rows, width), BF16),
-        vm((2, dp - 1, k_rows, width), BF16),
+        vm((2, dev, k_rows, width), BF16), vm((2, max(dev - 1, 1), k_rows, width), BF16),
         vm((2, k_rows, width), BF16), vm((2, k_rows, width), BF16),
         vm((seq, width), BF16), vm((seq, LANES), F32), vm((k_rows, width), BF16),
         vm((4 * k_rows, hid_own), BF16),
-        dma((3,)), dma((2,)), dma((2,)),
+        dma((3,)), dma((3,)), dma((2,)), dma((2,)), dma((2,)),
         *[dma((n, ny))] * 8,
         dma((dp - 1,)), dma((dp - 1,)),
-        dma((2, ex - 1)), dma((2, ex - 1)), dma((2, dp - 1)), dma((2, dp - 1)),
-        dma((2, dp - 1)), dma((2, dp - 1)), dma((2, ex - 1)), dma((2, ex - 1)),
-        dma((3,)), dma((3,)),
+        dma((2, ex - 1)), dma((2, ex - 1)), dma((2, ex, ny)), dma((2, ex, ny)),
+        dma((2, ex, dev)), dma((2, ex, dev)), dma((2, dev)), dma((2, dev)),
+        dma((2, ex, ny)), dma((2, ex, ny)), dma((2, ex - 1)), dma((2, ex - 1)),
+        dma((2 + ex,)), dma((2 + ex,)),
     ]
+    here, hbm = pl.BlockSpec(memory_space=pltpu.VMEM), pl.BlockSpec(memory_space=pl.ANY)
     result = pl.pallas_call(
         functools.partial(kernel, dp, ex, pieces),
         out_shape=jax.ShapeDtypeStruct((2, seq, width), BF16),
-        in_specs=[pl.BlockSpec(memory_space=pltpu.VMEM)] * 10,
-        out_specs=pl.BlockSpec(memory_space=pltpu.VMEM),
+        in_specs=[hbm, hbm, here, here, hbm, hbm, here, here, hbm, hbm],
+        out_specs=hbm,
         scratch_shapes=scratch,
         compiler_params=pltpu.CompilerParams(
             collective_id=0, has_side_effects=True, vmem_limit_bytes=60 * 2**20
         ),
     )(
-        inbound[0, 0], queued[0], routes[0, :, 0], gain_a, att_in[0], att_out[0], gain_b,
-        router[0], exp_in[0, 0], exp_out[0, 0],
+        inbound[0, 0], queued[0], routes[0, :, 0, :, 0], gain_a, att_in[0], att_out[0], gain_b,
+        router[0].T, exp_in[0, 0], exp_out[0, 0],
     )
     return result[None, :, None]
 

time: 90.8 us -> 78.5 us (0.86)
  Pallas kernels: 85.2 us -> 74.8 us
  local copies, waits for them, and re-layouts: 4.68 us -> 3.52 us
    pallas_call x1, Pallas kernels: 85.2 us -> 74.8 us  [per_device(): pl.pallas_call(functools.partial(kernel, dp, ex, pieces), out_shape=jax.S...]
    unnamed x6 -> x4, local copies, waits for them, and re-layouts: 3.84 us -> 3.52 us
where the time goes in v2:
time: 78.5 us; the launch traced here: 78.3 us
  Pallas kernels  74.8 us (95%)
  local copies, waits for them, and re-layouts  3.52 us (4%)
    pallas_call x1, Pallas kernels, per_device(): pl.pallas_call(functools.partial(kernel, dp, ex, pieces), out_shape=jax.S...  74.8 us
    unnamed x4, local copies, waits for them, and re-layouts  3.52 us

profile of v2, /device:TPU:0, one launch (start us, length us, event | category | flops | bytes accessed | tf_op | source)
XLA Modules:
  0.0 78.3 jit_solution(15449143169516640966)
XLA Ops:
  0.0 0.0 copy-start
  0.0 0.7 copy-done
  0.7 0.6 copy.14
  1.3 74.8 %shard_map.100 = bf16[2,256,1024]{2,1,0:T(8,128)(2,1)} custom-call(bf16[256,1024]{1,0:T(8,128)(2,1)} %bitcast.19, bf16[256,1024]{1,0:T(8,128)(2,1)} %bitcast.20, s32[2,256]{1,0:T(2,128)} %bitcast.23, f32[1,1024]{1,0:T(1,128)} %gain_a.1, bf16[256,1536]{1,0:T(8,128)(2,1)} %bitcast.18, bf16[128,1024]{1,0:T(8,128)(2,1)} %bitcast.21, f32[1,1024]{1,0:T(1,128)} %gain_b.1, ...), custom_call_target="tpu_custom_call" | custom-call | tf_op jit(solution)/shard_map/pallas_call | solution.py:364
  76.0 2.3 %copy.16 = bf16[1,2,1,256,1024]{4,3,2,1,0:T(8,128)(2,1)} copy(bf16[1,2,1,256,1024]{4,3,2,1,0:T(8,128)(2,1)} %bitcast.15) | data formatting | bytes 2097152
Async XLA Ops:
  0.0 0.7 copy-start

commit v3 on v2

--- a/solution.py
+++ b/solution.py
@@ -184,9 +184,11 @@
         else:
             source = entering
             loads[1].wait()
-            for i, view in enumerate(far_views):
+            for i, view in enumerate(far_views[:2]):
                 copy(view, view, x_s.at[i], x_r.at[i], {"section": far}).wait_recv()
             far_table = (slots.astype(F32) == far_gate[:, 1:2]).astype(F32)[:, :k_rows].astype(BF16)
+            for i, view in enumerate(far_views[2:]):
+                copy(view, view, x_s.at[2 + i], x_r.at[2 + i], {"section": far}).wait_recv()
             for j in range(0, width, 256):
                 at = slice(j, j + 256)
                 came = (far_mixed[:, at].astype(F32)
@@ -234,7 +236,6 @@
                 come = lax.rem(y - k + ny, ny) * 2 + c
                 view = rows.at[t, come, at]
                 copy(view, view, g_s.at[t, kk, k - 1], g_r.at[t, kk, k - 1], {"dp": come}).wait_recv()
-                send(view, view, h_s.at[t, kk, k], h_r.at[t, kk, k], {"dp": sib})
 
         for kk in range(ex):
             come = lax.rem(e - kk + ex, ex)
@@ -244,10 +245,11 @@
             for k in range(1, ny):
                 send(view, view, g_s.at[t, kk, k - 1], g_r.at[t, kk, k - 1],
                      {"dp": lax.rem(y + k, ny) * 2 + c})
+                send(view, view, h_s.at[t, kk, k], h_r.at[t, kk, k],
+                     {"dp": lax.rem(y + k, ny) * 2 + 1 - c})
             send(view, view, h_s.at[t, kk, 0], h_r.at[t, kk, 0], {"dp": sib})
-            if kk > 0:
-                pass_on(kk - 1)
-        pass_on(ex - 1)
+        for kk in range(ex):
+            pass_on(kk)
         if t == 0:
             own[2].wait()
             loads[2].wait()
@@ -336,7 +338,7 @@
     heads_w = att_out.shape[1] * dp
     cols = att_in.shape[2]
     in_rows, out_rows = att_in.shape[1], att_out.shape[1]
-    pieces = (max(1, min(4, in_rows // 32)), max(1, min(2, out_rows // 32)))
+    pieces = (max(1, min(8, in_rows // 32)), max(1, min(4, out_rows // 32)))
     n, ny = sum(pieces), max(dp // 2 - 1, 1)
     vm, dma = pltpu.VMEM, pltpu.SemaphoreType.DMA
     dev = dp // 2

time: 78.5 us -> 78.1 us (level)
  no operation moved by 1% of the time
where the time goes in v3:
time: 78.1 us; the launch traced here: 77.8 us
  Pallas kernels  74.3 us (95%)
  local copies, waits for them, and re-layouts  3.52 us (5%)
    pallas_call x1, Pallas kernels, per_device(): pl.pallas_call(functools.partial(kernel, dp, ex, pieces), out_shape=jax.S...  74.3 us
    unnamed x4, local copies, waits for them, and re-layouts  3.52 us

profile of v3, /device:TPU:0, one launch (start us, length us, event | category | flops | bytes accessed | tf_op | source)
XLA Modules:
  0.0 77.8 jit_solution(1028262791621699886)
XLA Ops:
  0.0 0.0 copy-start
  0.0 0.7 copy-done
  0.7 0.6 copy.14
  1.3 74.3 %shard_map.100 = bf16[2,256,1024]{2,1,0:T(8,128)(2,1)} custom-call(bf16[256,1024]{1,0:T(8,128)(2,1)} %bitcast.19, bf16[256,1024]{1,0:T(8,128)(2,1)} %bitcast.20, s32[2,256]{1,0:T(2,128)} %bitcast.23, f32[1,1024]{1,0:T(1,128)} %gain_a.1, bf16[256,1536]{1,0:T(8,128)(2,1)} %bitcast.18, bf16[128,1024]{1,0:T(8,128)(2,1)} %bitcast.21, f32[1,1024]{1,0:T(1,128)} %gain_b.1, ...), custom_call_target="tpu_custom_call" | custom-call | tf_op jit(solution)/shard_map/pallas_call | solution.py:366
  75.6 2.3 %copy.16 = bf16[1,2,1,256,1024]{4,3,2,1,0:T(8,128)(2,1)} copy(bf16[1,2,1,256,1024]{4,3,2,1,0:T(8,128)(2,1)} %bitcast.15) | data formatting | bytes 2097152
Async XLA Ops:
  0.0 0.7 copy-start
